TPU v7x, 32 devices: a whole 2x2x4 slice. The times are simulated.
32 devices in a mesh: row: 8 (over y, x, core), col: 4 (over z).
Axes of the slice: x: 2, y: 2, z: 4, core: 2. Of those that a mesh axis runs over, the one named last changes fastest.
Arguments:
- delta: float32 [4096, 4096], P('row', 'col'), may hold values from 0.5 to 64, as said below
- coords: float32 [4096, 64], P(('row', 'col')), may hold values from -6 to 6
- block_order: int32 [32], replicated, may hold values from 0 to 31, each once
Outputs:
- embedding: float32 [4096, 64], P(('row', 'col'))
- stress: float32 [4], replicated
Inputs may be any that keep to these rules, and one draw needn't show every extreme that they name: `delta`: symmetric, positive off the diagonal. `block_order`: each coordinate block once.
All inputs are finite; a program needn't handle non-finite values.
Results may differ from a plain program's by a relative error of at most 0.0003.
Values sent between devices are 32-bit elements; how exact they have to be, the bound alone decides.
A program may use at most 192 MiB of HBM per device.

v0:
```python
import jax
import jax.numpy as jnp
from jax import lax
from jax.sharding import PartitionSpec as P

ITERS = 4


def tile_update(tile, diagonal, row_coords, col_coords):
    gram = jnp.dot(
        row_coords,
        col_coords.T,
        precision=lax.Precision.HIGHEST,
        preferred_element_type=jnp.float32,
    )
    row_squares = jnp.sum(row_coords * row_coords, axis=1)
    col_squares = jnp.sum(col_coords * col_coords, axis=1)
    squared = row_squares[:, None] + col_squares[None, :] - 2.0 * gram
    distance = jnp.sqrt(jnp.where(diagonal, 1.0, squared) + 1e-06)
    ratio = jnp.where(diagonal, 0.0, tile / distance)
    partial_value = jnp.sum(ratio, axis=1)[:, None] * row_coords - jnp.dot(
        ratio, col_coords, precision=lax.Precision.HIGHEST, preferred_element_type=jnp.float32
    )
    misfit = jnp.sum(jnp.where(diagonal, 0.0, (tile - distance) ** 2))
    return (partial_value, misfit)


def body(delta, coords, block_order):
    block_size, dimensions = coords.shape
    row_devices = lax.axis_size("row")
    col_devices = lax.axis_size("col")
    row_count, col_count = delta.shape
    total_points = block_size * row_devices * col_devices
    stored = lax.all_gather(coords, ("row", "col"), axis=0, tiled=True)
    ordered = jnp.take(
        stored.reshape(row_devices * col_devices, block_size, dimensions), block_order, axis=0
    ).reshape(total_points, dimensions)
    row_place = lax.axis_index("row")
    col_place = lax.axis_index("col")
    row_start = row_place * row_count
    col_start = col_place * col_count
    row_coords = lax.dynamic_slice_in_dim(ordered, row_start, row_count, 0)
    col_coords = lax.dynamic_slice_in_dim(ordered, col_start, col_count, 0)
    diagonal = (row_start + jnp.arange(row_count))[:, None] == (col_start + jnp.arange(col_count))[
        None, :
    ]
    local_scale = jnp.sum(jnp.where(diagonal, 0.0, delta * delta))
    stresses = []
    share = coords
    for iteration in range(ITERS):
        more = iteration + 1 < ITERS
        partial_value, misfit = tile_update(delta, diagonal, row_coords, col_coords)
        share = (
            lax.psum_scatter(partial_value, "col", scatter_dimension=0, tiled=True) / total_points
        )
        misfit_total, scale_total = lax.psum((misfit, local_scale), ("row", "col"))
        stresses.append(misfit_total / scale_total)
        if more:
            gathered = lax.all_gather(share, ("row", "col"), axis=0, tiled=True)
            row_coords = lax.dynamic_slice_in_dim(gathered, row_start, row_count, 0)
            col_coords = lax.dynamic_slice_in_dim(gathered, col_start, col_count, 0)
    stress = jnp.stack(stresses)
    return (share, stress)


def solution(mesh):
    return jax.shard_map(
        body,
        mesh=mesh,
        in_specs=(P("row", "col"), P(("row", "col"), None), P()),
        out_specs=(P(("row", "col"), None), P()),
        check_vma=False,
    )
```

profile of v0, /device:TPU:0, one launch (start us, length us, event | category | flops | bytes accessed | tf_op | source)
XLA Modules:
  0.0 389.0 jit_solution(16535859305902919494)
XLA Ops:
  9.4 56.7 %all-gather.5.cloned.1.call-done = f32[4096,64]{0,1:T(8,128)} async-done(((f32[128,64]{0,1:T(8,128)}), f32[4096,64]{0,1:T(8,128)}) %all-gather.5.cloned.1.call-update) | async-done | bytes 1048592 | tf_op jit(solution)/shard_map/all_gather | solution.py:34
  66.1 1.3 copy_bitcast_fusion
  68.3 1.4 copy-done
  69.7 4.5 %fusion.36 = (f32[512]{0:T(512)S(1)}, f32[512,1024]{1,0:T(8,128)S(1)}, f32[512,1024]{1,0:T(8,128)}) fusion(f32[512,1024]{1,0:T(8,128)S(1)} %copy-done, s32[1024]{0:T(1024)S(1)} %iota_add_fusion, s32[512]{0:T(512)S(1)} %iota_add_fusion.1, f32[4096,64]{0,1:T(8,128)S(1)} %bitcast_select_fusion, s32[]{:T(128)S(6)} %select_n.65, s32[]{:T(128)S(6)} %select_n.64, ...), kind=kOutput, calls=%fused_computation.75 | convolution fusion | flops 407371264 | bytes 6699016 | tf_op jit(solution)/shard_map/dot_general | solution.py:10
  74.2 2.8 convolution_subtract_fusion.3
  77.1 19.2 %reduce-scatter.5.cloned.1.call-done = f32[128,64]{0,1:T(8,128)} async-done(((f32[512,64]{0,1:T(8,128)}), f32[128,64]{0,1:T(8,128)}) %reduce-scatter.5.cloned.1.call-update) | async-done | bytes 32784 | tf_op jit(solution)/shard_map/reduce_scatter | solution.py:54
  96.3 1.4 broadcast_multiply_fusion.3
  97.7 53.1 %all-gather.7.cloned.1.call-done = f32[4096,64]{0,1:T(8,128)} async-done(((f32[128,64]{0,1:T(8,128)}), f32[4096,64]{0,1:T(8,128)}) %all-gather.7.cloned.1.call-update) | async-done | bytes 1048592 | tf_op jit(solution)/shard_map/all_gather | solution.py:59
  151.8 1.0 multiply_reduce_fusion.2
  152.8 5.5 %fusion.35 = (f32[512]{0:T(512)S(1)}, f32[512,1024]{1,0:T(8,128)S(1)}, f32[512,1024]{1,0:T(8,128)}) fusion(f32[512,1024]{1,0:T(8,128)S(1)} %copy-done.1, s32[1024]{0:T(1024)S(1)} %iota_add_fusion, s32[512]{0:T(512)S(1)} %iota_add_fusion.1, f32[4096,64]{0,1:T(8,128)} %all-gather.7.cloned.1.call-done, s32[]{:T(128)S(6)} %select_n.65, s32[]{:T(128)S(6)} %select_n.64, ...), kind=kOutput, calls=%fused_computation.74 | convolution fusion | flops 407371264 | bytes 6699016 | tf_op jit(solution)/shard_map/dot_general | solution.py:10
  158.3 3.8 convolution_subtract_fusion.2
  162.1 19.2 %reduce-scatter.7.cloned.1.call-done = f32[128,64]{0,1:T(8,128)} async-done(((f32[512,64]{0,1:T(8,128)}), f32[128,64]{0,1:T(8,128)}) %reduce-scatter.7.cloned.1.call-update) | async-done | bytes 32784 | tf_op jit(solution)/shard_map/reduce_scatter | solution.py:54
  181.3 1.4 broadcast_multiply_fusion.2
  182.9 52.4 %all-gather.9.cloned.1.call-done = f32[4096,64]{0,1:T(8,128)} async-done(((f32[128,64]{0,1:T(8,128)}), f32[4096,64]{0,1:T(8,128)}) %all-gather.9.cloned.1.call-update) | async-done | bytes 1048592 | tf_op jit(solution)/shard_map/all_gather | solution.py:59
  236.2 1.0 multiply_reduce_fusion.1
  237.2 5.5 %fusion.34 = (f32[512]{0:T(512)S(1)}, f32[512,1024]{1,0:T(8,128)S(1)}, f32[512,1024]{1,0:T(8,128)}) fusion(f32[512,1024]{1,0:T(8,128)S(1)} %copy-done.1, s32[1024]{0:T(1024)S(1)} %iota_add_fusion, s32[512]{0:T(512)S(1)} %iota_add_fusion.1, f32[4096,64]{0,1:T(8,128)} %all-gather.9.cloned.1.call-done, s32[]{:T(128)S(6)} %select_n.65, s32[]{:T(128)S(6)} %select_n.64, ...), kind=kOutput, calls=%fused_computation.73 | convolution fusion | flops 407371264 | bytes 6699016 | tf_op jit(solution)/shard_map/dot_general | solution.py:10
  242.8 3.8 convolution_subtract_fusion.1
  246.6 19.2 %reduce-scatter.9.cloned.1.call-done = f32[128,64]{0,1:T(8,128)} async-done(((f32[512,64]{0,1:T(8,128)}), f32[128,64]{0,1:T(8,128)}) %reduce-scatter.9.cloned.1.call-update) | async-done | bytes 32784 | tf_op jit(solution)/shard_map/reduce_scatter | solution.py:54
  265.8 1.4 broadcast_multiply_fusion.1
  267.3 53.1 %all-gather.11.cloned.1.call-done = f32[4096,64]{0,1:T(8,128)} async-done(((f32[128,64]{0,1:T(8,128)}), f32[4096,64]{0,1:T(8,128)}) %all-gather.11.cloned.1.call-update) | async-done | bytes 1048592 | tf_op jit(solution)/shard_map/all_gather | solution.py:59
  322.3 8.3 %fusion.8 = (f32[]{:T(128)}, f32[]{:T(128)}, f32[]{:T(128)}, f32[]{:T(128)}, f32[]{:T(128)}, /*index=5*/f32[512]{0:T(512)S(1)}, f32[512,1024]{1,0:T(8,128)S(1)}) fusion(f32[512,1024]{1,0:T(8,128)S(1)} %copy-done.1, f32[512,1024]{1,0:T(8,128)} %get-tuple-element.22, s32[1024]{0:T(1024)S(1)} %iota_add_fusion, s32[512]{0:T(512)S(1)} %iota_add_fusion.1, ...), kind=kOutput, calls=%fused_computation.22 | convolution fusion | flops 417332736 | bytes 10893340 | tf_op jit(solution)/shard_map/dot_general | solution.py:10
  330.6 3.8 convolution_subtract_fusion
  334.4 40.5 %all-reduce = (f32[]{:T(128)}, f32[]{:T(128)}, f32[]{:T(128)}, f32[]{:T(128)}, f32[]{:T(128)}) all-reduce(f32[]{:T(128)} %get-tuple-element.5, f32[]{:T(128)} %get-tuple-element.4, f32[]{:T(128)} %get-tuple-element.6, f32[]{:T(128)} %get-tuple-element.3, f32[]{:T(128)} %get-tuple-element.2), channel_id=1, replica_groups=mesh['row'=8,'col'=4] {'row','col'}, use_global_device_ids=true, to_apply=%region_25.26 | all-reduce | flops 5 | bytes 40 | tf_op jit(solution)/shard_map/psum | solution.py:56
  380.7 1.4 broadcast_multiply_fusion
  (35 shorter events, 7.9 us)
Async XLA Ops:
  7.2 59.0 %all-gather.5.cloned.1.call-start = ((), (), s32[]{:S(2)}) async-start(), calls=%async_computation.4 | async-start | bytes 1081344 | tf_op jit(solution)/shard_map/all_gather | solution.py:34
  7.9 88.4 %reduce-scatter.5.cloned.1.call-start = ((), (), s32[]{:S(2)}) async-start(), calls=%async_computation.5 | async-start | bytes 163840 | tf_op jit(solution)/shard_map/reduce_scatter | solution.py:54
  68.1 1.6 copy-start
  74.2 78.6 %copy-start.1 = (f32[512,1024]{1,0:T(8,128)S(1)}, f32[512,1024]{1,0:T(8,128)}, u32[]{:S(2)}) copy-start(f32[512,1024]{1,0:T(8,128)} %param.3) | copy-start | bytes 6291460
  77.0 73.8 %all-gather.7.cloned.1.call-start = ((), (), s32[]{:S(2)}) async-start(), calls=%async_computation.6 | async-start | bytes 1081344 | tf_op jit(solution)/shard_map/all_gather | solution.py:59
  97.7 83.6 %reduce-scatter.7.cloned.1.call-start = ((), (), s32[]{:S(2)}) async-start(), calls=%async_computation.7 | async-start | bytes 163840 | tf_op jit(solution)/shard_map/reduce_scatter | solution.py:54
  162.1 73.3 %all-gather.9.cloned.1.call-start = ((), (), s32[]{:S(2)}) async-start(), calls=%async_computation.8 | async-start | bytes 1081344 | tf_op jit(solution)/shard_map/all_gather | solution.py:59
  182.7 83.1 %reduce-scatter.9.cloned.1.call-start = ((), (), s32[]{:S(2)}) async-start(), calls=%async_computation.9 | async-start | bytes 163840 | tf_op jit(solution)/shard_map/reduce_scatter | solution.py:54
  246.6 73.8 %all-gather.11.cloned.1.call-start = ((), (), s32[]{:S(2)}) async-start(), calls=%async_computation.10 | async-start | bytes 1081344 | tf_op jit(solution)/shard_map/all_gather | solution.py:59
  267.2 113.5 %reduce-scatter.11.cloned.1.call-start = ((), (), s32[]{:S(2)}) async-start(), calls=%async_computation.11 | async-start | bytes 163840 | tf_op jit(solution)/shard_map/reduce_scatter | solution.py:54
Sparse Core Ops, SparseCore 0:
  10.9 55.1 all-gather.4
  77.1 19.0 reduce-scatter.4
  100.2 50.6 all-gather.6
  162.2 19.0 reduce-scatter.6
  184.6 50.6 all-gather.8
  246.7 19.0 reduce-scatter.8
  269.7 50.6 all-gather.10
  334.5 19.1 reduce-scatter.10
where the time goes:
time: 390 us; the launch traced here: 389 us
  waiting for transfers between devices  274 us (70%)
  blocking collectives  40.5 us (10%)
  matrix products  38 us (10%)
  between operations  19.5 us (5%)
  other arithmetic  13.3 us (3%)
    all_gather x3, waiting for transfers between devices, body(): gathered = lax.all_gather(share, ('row', 'col'), axis=0, tiled=True)  159 us
    reduce_scatter x4, waiting for transfers between devices, body(): lax.psum_scatter(partial_value, 'col', scatter_dimension=0, tiled=True)  57.6 us
    all_gather x1, waiting for transfers between devices, body(): stored = lax.all_gather(coords, ('row', 'col'), axis=0, tiled=True)  56.7 us
    psum x1, blocking collectives, body(): misfit_total, scale_total = lax.psum((misfit, local_scale), ('row', 'col'))  40.5 us
    dot_general x4, matrix products, tile_update(): jnp.dot(row_coords, col_coords.T, precision=lax.Precision.HIGHEST, prefer...  23.9 us
    dot_general x4, matrix products, tile_update(): jnp.dot(ratio, col_coords, precision=lax.Precision.HIGHEST, preferred_ele...  14.1 us
  transfers between devices with their start and end apart: 8, of which 7 were waited for; matrix products, arithmetic and copies ran while one was open for 1% of the time, Pallas kernels for 0%

commit v1 on v0

v1 whole, which is shorter than its diff:
```python
import functools

import jax
import jax.numpy as jnp
from jax import lax
from jax.experimental import pallas as pl
from jax.experimental.pallas import tpu as pltpu
from jax.sharding import PartitionSpec as P

ITERS = 4
MESH = pl.DeviceIdType.MESH
F32 = jnp.float32
BF16 = jnp.bfloat16
STEP = 256


class Exchange:
    def __init__(self, axis, size, send_sem, recv_sem):
        self.axis, self.size = axis, size
        self.me = lax.axis_index(axis)
        self.send_sem, self.recv_sem = send_sem, recv_sem

    def peer(self, offset):
        return lax.rem(self.me + offset, self.size)

    def copy(self, src, dst, peer, slot):
        return pltpu.make_async_remote_copy(
            src_ref=src,
            dst_ref=dst,
            send_sem=self.send_sem.at[peer],
            recv_sem=self.recv_sem.at[slot],
            device_id={self.axis: peer},
            device_id_type=MESH,
        )

    def start_scatter(self, chunks, landing):
        for offset in range(1, self.size):
            peer = self.peer(offset)
            self.copy(chunks.at[peer], landing.at[self.me], peer, self.me).start()

    def start_gather(self, blocks):
        for offset in range(1, self.size):
            peer = self.peer(offset)
            self.copy(blocks.at[self.me], blocks.at[self.me], peer, self.me).start()

    def wait_recv(self, landing):
        for offset in range(1, self.size):
            peer = self.peer(offset)
            self.copy(landing.at[peer], landing.at[peer], peer, peer).wait_recv()

    def wait_send(self, chunks):
        for offset in range(1, self.size):
            peer = self.peer(offset)
            self.copy(chunks.at[peer], chunks.at[peer], peer, peer).wait_send()


def fold(values):
    rows, cols = values.shape
    tall = jnp.sum(values.reshape(rows // 8, 8, cols), axis=0)
    total = tall[:, :128]
    for start in range(128, cols, 128):
        total = total + tall[:, start : start + 128]
    return total


def split(block):
    high = block.astype(BF16)
    low = (block - high.astype(F32)).astype(BF16)
    return high, low


def kernel(
    n_row,
    n_col,
    order_ref,
    delta_hbm,
    coords_ref,
    out_ref,
    stress_ref,
    delta,
    rat_hi,
    rat_lo,
    left,
    right,
    w_row,
    w_col,
    sq_row,
    sq_col,
    acc_row,
    acc_col,
    chunks_r,
    chunks_c,
    land_r,
    land_c,
    ag_r,
    ag_c,
    fin,
    misfit_acc,
    totals,
    delta_sem,
    sems_r,
    sems_c,
):
    blk, dim = coords_ref.shape
    rows, cols = delta.shape
    points = blk * n_row * n_col
    rs_r = Exchange("col", n_col, sems_r.at[0], sems_r.at[1])
    gt_r = Exchange("col", n_col, sems_r.at[2], sems_r.at[3])
    rs_c = Exchange("row", n_row, sems_c.at[0], sems_c.at[1])
    gt_c = Exchange("row", n_row, sems_c.at[2], sems_c.at[3])
    fn_c = Exchange("row", n_row, sems_c.at[4], sems_c.at[5])
    r, c = rs_c.me, rs_r.me

    load = pltpu.make_async_copy(delta_hbm, delta, delta_sem)
    load.start()

    barrier = pltpu.get_barrier_semaphore()
    for exchange in (rs_r, rs_c):
        for offset in range(1, exchange.size):
            pl.semaphore_signal(
                barrier, inc=1, device_id={exchange.axis: exchange.peer(offset)}, device_id_type=MESH
            )
    own = coords_ref[...].T
    ag_r[c] = own
    ag_c[r, 0:dim] = own
    ag_c[r, dim : dim + 8] = jnp.zeros((8, 128), F32)
    pl.semaphore_wait(barrier, n_row + n_col - 2)

    gt_r.start_gather(ag_r)
    gt_c.start_gather(ag_c)

    load.wait()
    misfit_acc[...] = jnp.zeros((8, 128), F32)
    w_row[2 * dim :] = jnp.ones((16, rows), BF16)
    w_col[2 * dim :] = jnp.ones((16, cols), BF16)

    def scale_step(step, carry):
        at = pl.ds(pl.multiple_of(step * STEP, STEP), STEP)
        tile = delta[:, at]
        row_id = r * rows + lax.broadcasted_iota(jnp.int32, tile.shape, 0)
        col_id = c * cols + step * STEP + lax.broadcasted_iota(jnp.int32, tile.shape, 1)
        tile = jnp.where(row_id == col_id, 0.0, tile)
        delta[:, at] = tile
        misfit_acc[...] += fold(tile * tile)
        return carry

    lax.fori_loop(0, cols // STEP, scale_step, 0)

    gt_r.wait_recv(ag_r)
    gt_c.wait_recv(ag_c)
    gt_r.wait_send(ag_r)
    gt_c.wait_send(ag_c)

    for k in range(n_col):
        stored = order_ref[r * n_col + k]
        here = lax.rem(stored, n_col) == c
        chunks_r[k, 0:dim] = jnp.where(here, ag_c[lax.div(stored, n_col), 0:dim], 0.0)
        chunks_r[k, dim : dim + 8] = misfit_acc[...]
    for k in range(n_row):
        stored = order_ref[c * n_row + k]
        here = lax.div(stored, n_col) == r
        chunks_c[k] = jnp.where(here, ag_r[lax.rem(stored, n_col)], 0.0)
    rs_r.start_scatter(chunks_r, land_r)
    rs_c.start_scatter(chunks_c, land_c)

    def reduced_row(factor):
        rs_r.wait_recv(land_r)
        total = chunks_r[c]
        for offset in range(1, n_col):
            total = total + land_r[rs_r.peer(offset)]
        return total[0:dim] * factor, total[dim : dim + 8]

    def finish(number, factor):
        share, misfit = reduced_row(factor)
        ag_r[c] = share
        gt_r.start_gather(ag_r)
        rs_c.wait_recv(land_c)
        total = chunks_c[r]
        for offset in range(1, n_row):
            total = total + land_c[rs_c.peer(offset)]
        ag_c[r, 0:dim] = total * factor
        ag_c[r, dim : dim + 8] = misfit
        gt_c.start_gather(ag_c)
        rs_r.wait_send(chunks_r)
        rs_c.wait_send(chunks_c)

        gt_r.wait_recv(ag_r)
        for k in range(n_col):
            at = slice(k * blk, (k + 1) * blk)
            high, low = split(ag_r[k])
            w_row[0:dim, at] = high
            w_row[dim : 2 * dim, at] = low
            high, low = high.astype(F32), low.astype(F32)
            kept = high + low
            stacked = jnp.concatenate([high, high, low, low], axis=0) * -2.0
            left[at, :] = stacked.T.astype(BF16)
            sq_row[at, :] = jnp.sum(kept * kept, axis=0, keepdims=True).T
        gt_c.wait_recv(ag_c)
        grand = jnp.zeros((8, 128), F32)
        for k in range(n_row):
            at = slice(k * blk, (k + 1) * blk)
            high, low = split(ag_c[k, 0:dim])
            w_col[0:dim, at] = high
            w_col[dim : 2 * dim, at] = low
            right[0:dim, at] = high
            right[dim : 2 * dim, at] = low
            right[2 * dim : 3 * dim, at] = high
            right[3 * dim : 4 * dim, at] = low
            kept = high.astype(F32) + low.astype(F32)
            sq_col[:, at] = jnp.sum(kept * kept, axis=0, keepdims=True) + 1e-06
            grand = grand + ag_c[k, dim : dim + 8]
        totals[number] = grand
        gt_r.wait_send(ag_r)
        gt_c.wait_send(ag_c)

    def row_sums():
        acc_row[...] = jnp.zeros_like(acc_row)
        misfit_acc[...] = jnp.zeros((8, 128), F32)

        def step_body(step, carry):
            at = pl.ds(pl.multiple_of(step * STEP, STEP), STEP)
            gram = jnp.dot(left[...], right[:, at], preferred_element_type=F32)
            squared = jnp.maximum(sq_row[...] + sq_col[:, at] + gram, 1e-06)
            inverse = lax.rsqrt(squared)
            tile = delta[:, at]
            error = jnp.where(tile > 0.0, tile - squared * inverse, 0.0)
            misfit_acc[...] += fold(error * error)
            high, low = split(tile * inverse)
            rat_hi[:, at] = high
            rat_lo[:, at] = low
            weights = w_col[:, at]
            contract = (((1,), (1,)), ((), ()))
            acc_row[...] += lax.dot_general(
                weights, high, contract, preferred_element_type=F32
            ) + lax.dot_general(weights, low, contract, preferred_element_type=F32)
            return carry

        lax.fori_loop(0, cols // STEP, step_body, 0)
        misfit = misfit_acc[...]
        for k in range(n_col):
            at = slice(k * blk, (k + 1) * blk)
            kept = w_row[0:dim, at].astype(F32) + w_row[dim : 2 * dim, at].astype(F32)
            chunks_r[k, 0:dim] = acc_row[2 * dim : 2 * dim + 1, at] * kept - (
                acc_row[0:dim, at] + acc_row[dim : 2 * dim, at]
            )
            chunks_r[k, dim : dim + 8] = misfit
        rs_r.start_scatter(chunks_r, land_r)

    def col_sums():
        def step_body(step, carry):
            at = pl.ds(pl.multiple_of(step * STEP, STEP), STEP)
            acc_col[:, at] = jnp.dot(
                w_row[...], rat_hi[:, at], preferred_element_type=F32
            ) + jnp.dot(w_row[...], rat_lo[:, at], preferred_element_type=F32)
            return carry

        lax.fori_loop(0, cols // STEP, step_body, 0)
        for k in range(n_row):
            at = slice(k * blk, (k + 1) * blk)
            kept = w_col[0:dim, at].astype(F32) + w_col[dim : 2 * dim, at].astype(F32)
            chunks_c[k] = acc_col[2 * dim : 2 * dim + 1, at] * kept - (
                acc_col[0:dim, at] + acc_col[dim : 2 * dim, at]
            )
        rs_c.start_scatter(chunks_c, land_c)

    finish(0, 1.0)

    def iteration(number, carry):
        row_sums()
        col_sums()
        finish(number, 1.0 / points)
        return carry

    lax.fori_loop(1, ITERS, iteration, 0)
    row_sums()
    share, misfit = reduced_row(1.0 / points)
    fin[r] = misfit
    fn_c.start_gather(fin)
    out_ref[...] = share.T
    rs_r.wait_send(chunks_r)
    fn_c.wait_recv(fin)
    grand = fin[0]
    for k in range(1, n_row):
        grand = grand + fin[k]
    totals[ITERS] = grand
    fn_c.wait_send(fin)
    scale = jnp.sum(totals[0], keepdims=True)
    for number in range(ITERS):
        stress_ref[number] = (jnp.sum(totals[number + 1], keepdims=True) / scale)[0, 0]


def body(n_row, n_col, delta, coords, block_order):
    blk, dim = coords.shape
    rows, cols = delta.shape
    vmem = pl.BlockSpec(memory_space=pltpu.VMEM)
    return pl.pallas_call(
        functools.partial(kernel, n_row, n_col),
        out_shape=(
            jax.ShapeDtypeStruct((blk, dim), F32),
            jax.ShapeDtypeStruct((ITERS,), F32),
        ),
        in_specs=[
            pl.BlockSpec(memory_space=pltpu.SMEM),
            pl.BlockSpec(memory_space=pl.ANY),
            vmem,
        ],
        out_specs=(vmem, pl.BlockSpec(memory_space=pltpu.SMEM)),
        scratch_shapes=[
            pltpu.VMEM((rows, cols), F32),
            pltpu.VMEM((rows, cols), BF16),
            pltpu.VMEM((rows, cols), BF16),
            pltpu.VMEM((rows, 4 * dim), BF16),
            pltpu.VMEM((4 * dim, cols), BF16),
            pltpu.VMEM((2 * dim + 16, rows), BF16),
            pltpu.VMEM((2 * dim + 16, cols), BF16),
            pltpu.VMEM((rows, 1), F32),
            pltpu.VMEM((1, cols), F32),
            pltpu.VMEM((2 * dim + 16, rows), F32),
            pltpu.VMEM((2 * dim + 16, cols), F32),
            pltpu.VMEM((n_col, dim + 8, blk), F32),
            pltpu.VMEM((n_row, dim, blk), F32),
            pltpu.VMEM((n_col, dim + 8, blk), F32),
            pltpu.VMEM((n_row, dim, blk), F32),
            pltpu.VMEM((n_col, dim, blk), F32),
            pltpu.VMEM((n_row, dim + 8, blk), F32),
            pltpu.VMEM((n_row, 8, 128), F32),
            pltpu.VMEM((8, 128), F32),
            pltpu.VMEM((ITERS + 1, 8, 128), F32),
            pltpu.SemaphoreType.DMA,
            pltpu.SemaphoreType.DMA((4, n_col)),
            pltpu.SemaphoreType.DMA((6, n_row)),
        ],
        compiler_params=pltpu.CompilerParams(
            collective_id=0, has_side_effects=True, vmem_limit_bytes=48 * 1024 * 1024
        ),
    )(block_order, delta, coords)


def solution(mesh):
    sizes = dict(mesh.shape)
    return jax.shard_map(
        functools.partial(body, sizes["row"], sizes["col"]),
        mesh=mesh,
        in_specs=(P("row", "col"), P(("row", "col"), None), P()),
        out_specs=(P(("row", "col"), None), P()),
        check_vma=False,
    )
```

time: 390 us -> 81 us (0.21)
  waiting for transfers between devices: 274 us -> 0 us
  Pallas kernels: 0 us -> 75.8 us
  blocking collectives: 40.5 us -> 0 us
  matrix products: 38 us -> 0 us
  between operations: 19.5 us -> 0.65 us
  other arithmetic: 13.3 us -> 0 us
    all_gather x4 -> x0, waiting for transfers between devices: 215 us -> none  [the longest x3 159 us: body(): gathered = lax.all_gather(share, ('row', 'col'), axis=0, tiled=True)]
    pallas_call x0 -> x1, Pallas kernels: none -> 75.8 us  [body(): pl.pallas_call(functools.partial(kernel, n_row, n_col), out_shape=(jax.Sh...]
    reduce_scatter x4 -> x0, waiting for transfers between devices: 57.6 us -> none  [body(): lax.psum_scatter(partial_value, 'col', scatter_dimension=0, tiled=True)]
    psum x1 -> x0, blocking collectives: 40.5 us -> none  [body(): misfit_total, scale_total = lax.psum((misfit, local_scale), ('row', 'col'))]
    dot_general x8 -> x0, matrix products: 38 us -> none  [the longest x4 23.9 us: tile_update(): jnp.dot(row_coords, col_coords.T, precision=lax.Precision.HIGHEST, prefer...]
    reduce_sum x8 -> x0, other arithmetic: 5.82 us -> none  [the longest x4 2.99 us: tile_update(): col_squares = jnp.sum(col_coords * col_coords, axis=1)]
    div x4 -> x0, other arithmetic: 5.5 us -> none  [body(): lax.psum_scatter(partial_value, 'col', scatter_dimension=0, tiled=True)]
  transfers between devices with their start and end apart: 8 -> 0, of which waited for: 7 -> 0; matrix products, arithmetic and copies ran while one was open for 1% -> 0% of each run, Pallas kernels for 0% -> 0%
where the time goes in v1:
time: 81 us; the launch traced here: 80.8 us
  Pallas kernels  75.8 us (94%)
  local copies, waits for them, and re-layouts  4.3 us (5%)
    pallas_call x1, Pallas kernels, body(): pl.pallas_call(functools.partial(kernel, n_row, n_col), out_shape=(jax.Sh...  75.8 us
    unnamed x6, local copies, waits for them, and re-layouts  3.6 us

profile of v1, /device:TPU:0, one launch (start us, length us, event | category | flops | bytes accessed | tf_op | source)
XLA Modules:
  0.0 80.8 jit_solution(419389449509733256)
XLA Ops:
  0.6 0.8 %copy.5.coords_ref = f32[128,64]{1,0:T(8,128)S(1)} copy(f32[128,64]{0,1:T(8,128)} %param.4) | data formatting | bytes 65536 | tf_op args[1]
  1.5 0.0 copy-start
  1.5 1.6 %copy-done = f32[512,1024]{1,0:T(8,128)S(1)} copy-done((f32[512,1024]{1,0:T(8,128)S(1)}, f32[512,1024]{1,0:T(8,128)}, u32[]{:S(2)}) %copy-start) | copy-done | bytes 2097176
  3.1 0.0 copy-start.1
  3.1 0.7 copy-done.1
  3.7 75.8 %shard_map.50 = (f32[128,64]{1,0:T(8,128)S(1)}, f32[4]{0:T(128)S(1)}) custom-call(s32[32]{0:T(128)S(1)} %copy-done.1, f32[512,1024]{1,0:T(8,128)S(1)} %copy-done, f32[128,64]{1,0:T(8,128)S(1)} %copy.5.coords_ref), custom_call_target="tpu_custom_call" | custom-call | tf_op jit(solution)/shard_map/pallas_call | solution.py:296
  79.6 0.7 copy.6
  80.3 0.5 copy.8
Async XLA Ops:
  1.5 1.6 %copy-start = (f32[512,1024]{1,0:T(8,128)S(1)}, f32[512,1024]{1,0:T(8,128)}, u32[]{:S(2)}) copy-start(f32[512,1024]{1,0:T(8,128)} %delta_hbm.1) | copy-start | bytes 6291460
  3.1 0.7 copy-start.1

commit v2 on v1

v2 whole, which is shorter than its diff:
```python
import functools

import jax
import jax.numpy as jnp
from jax import lax
from jax.experimental import pallas as pl
from jax.experimental.pallas import tpu as pltpu
from jax.sharding import PartitionSpec as P

ITERS = 4
MESH = pl.DeviceIdType.MESH
F32 = jnp.float32
BF16 = jnp.bfloat16
STEP = 512
UNROLL = False


class Exchange:
    def __init__(self, axis, size, send_sem, recv_sem):
        self.axis, self.size = axis, size
        self.me = lax.axis_index(axis)
        self.send_sem, self.recv_sem = send_sem, recv_sem

    def peer(self, offset):
        return lax.rem(self.me + offset, self.size)

    def copy(self, src, dst, peer, slot):
        return pltpu.make_async_remote_copy(
            src_ref=src,
            dst_ref=dst,
            send_sem=self.send_sem.at[peer],
            recv_sem=self.recv_sem.at[slot],
            device_id={self.axis: peer},
            device_id_type=MESH,
        )

    def start_scatter(self, chunks, landing):
        for offset in range(1, self.size):
            peer = self.peer(offset)
            self.copy(chunks.at[peer], landing.at[self.me], peer, self.me).start()

    def start_gather(self, blocks):
        for offset in range(1, self.size):
            peer = self.peer(offset)
            self.copy(blocks.at[self.me], blocks.at[self.me], peer, self.me).start()

    def wait_recv(self, landing):
        for offset in range(1, self.size):
            peer = self.peer(offset)
            self.copy(landing.at[peer], landing.at[peer], peer, peer).wait_recv()

    def wait_one(self, landing, peer):
        self.copy(landing.at[peer], landing.at[peer], peer, peer).wait_recv()

    def wait_send(self, chunks):
        for offset in range(1, self.size):
            peer = self.peer(offset)
            self.copy(chunks.at[peer], chunks.at[peer], peer, peer).wait_send()


def fold(values):
    rows, cols = values.shape
    tall = jnp.sum(values.reshape(rows // 8, 8, cols), axis=0)
    total = tall[:, :128]
    for start in range(128, cols, 128):
        total = total + tall[:, start : start + 128]
    return total


def split(block):
    high = block.astype(BF16)
    low = (block - high.astype(F32)).astype(BF16)
    return high, low


def kernel(
    n_row,
    n_col,
    order_ref,
    delta_hbm,
    coords_ref,
    out_ref,
    stress_ref,
    delta,
    left,
    right,
    w_row,
    w_col,
    sq_row,
    sq_col,
    acc_row,
    chunks_r,
    chunks_c,
    land_r,
    land_c,
    ag_r,
    ag_c,
    fin_r,
    fin_c,
    misfit_acc,
    scale_acc,
    pool,
    totals,
    delta_sem,
    pool_sem,
    line_sem,
    plane_sem,
    twin_sem,
    sems_r,
    sems_c,
):
    blk, dim = coords_ref.shape
    rows, cols = delta.shape
    points = blk * n_row * n_col
    rs_r = Exchange("col", n_col, sems_r.at[0], sems_r.at[1])
    gt_r = Exchange("col", n_col, sems_r.at[2], sems_r.at[3])
    rs_c = Exchange("row", n_row, sems_c.at[0], sems_c.at[1])
    gt_c = Exchange("row", n_row, sems_c.at[2], sems_c.at[3])
    fn_r = Exchange("col", n_col, sems_r.at[4], sems_r.at[5])
    fn_c = Exchange("row", n_row, sems_c.at[4], sems_c.at[5])
    r, c = rs_c.me, rs_r.me

    load = pltpu.make_async_copy(delta_hbm, delta, delta_sem)
    load.start()

    barrier = pltpu.get_barrier_semaphore()
    for exchange in (rs_r, rs_c):
        for offset in range(1, exchange.size):
            pl.semaphore_signal(
                barrier, inc=1, device_id={exchange.axis: exchange.peer(offset)}, device_id_type=MESH
            )
    twin = r + 1 - 2 * lax.rem(r, 2)
    own = r * n_col + c
    pool[own] = coords_ref[...].T
    pl.semaphore_wait(barrier, n_row + n_col - 2)

    def pass_on(slot, device, sem):
        return pltpu.make_async_remote_copy(
            src_ref=pool.at[slot],
            dst_ref=pool.at[slot],
            send_sem=sem,
            recv_sem=pool_sem.at[slot],
            device_id=device,
            device_id_type=MESH,
        )

    def arrived(slot):
        pass_on(slot, {"row": twin}, twin_sem.at[0, 0]).wait_recv()

    sent = []

    def send_on(*args):
        copy = pass_on(*args)
        copy.start()
        sent.append(copy)

    lines = n_row // 2
    for offset in range(1, n_col):
        send_on(own, {"col": rs_r.peer(offset)}, line_sem.at[offset])

    def spread(offset):
        slot = r * n_col + rs_r.peer(offset)
        for k in range(1, lines):
            send_on(slot, {"row": rs_c.peer(2 * k)}, plane_sem.at[k, offset])
        send_on(slot, {"row": twin}, twin_sem.at[0, offset])

    spread(0)

    load.wait()
    scale_acc[...] = jnp.zeros((8, 128), F32)
    w_row[2 * dim :] = jnp.ones((16, rows), BF16)
    w_col[2 * dim :] = jnp.ones((16, cols), BF16)

    def scale_step(step, carry):
        at = pl.ds(pl.multiple_of(step * STEP, STEP), STEP)
        tile = delta[:, at]
        row_id = r * rows + lax.broadcasted_iota(jnp.int32, tile.shape, 0)
        col_id = c * cols + step * STEP + lax.broadcasted_iota(jnp.int32, tile.shape, 1)
        tile = jnp.where(row_id == col_id, 0.0, tile)
        delta[:, at] = tile
        scale_acc[...] += fold(tile * tile)
        return carry

    lax.fori_loop(0, cols // STEP, scale_step, 0)

    for offset in range(1, n_col):
        arrived(r * n_col + rs_r.peer(offset))
        spread(offset)
    for offset in range(n_col):
        for k in range(1, lines):
            slot = rs_c.peer(2 * k) * n_col + rs_r.peer(offset)
            arrived(slot)
            send_on(slot, {"row": twin}, twin_sem.at[k, offset])
    for offset in range(n_col):
        for k in range(lines):
            arrived(lax.rem(twin + 2 * k, n_row) * n_col + rs_r.peer(offset))

    def prepare_row(k, block):
        at = pl.ds(pl.multiple_of(k * blk, blk), blk)
        high, low = split(block)
        w_row[0:dim, at] = high
        w_row[dim : 2 * dim, at] = low
        high, low = high.astype(F32), low.astype(F32)
        kept = high + low
        stacked = jnp.concatenate([high, high, low, low], axis=0) * -2.0
        left[at, :] = stacked.T.astype(BF16)
        sq_row[at, :] = jnp.sum(kept * kept, axis=0, keepdims=True).T

    def prepare_col(k, block):
        at = pl.ds(pl.multiple_of(k * blk, blk), blk)
        high, low = split(block)
        w_col[0:dim, at] = high
        w_col[dim : 2 * dim, at] = low
        right[0:dim, at] = high
        right[dim : 2 * dim, at] = low
        right[2 * dim : 3 * dim, at] = high
        right[3 * dim : 4 * dim, at] = low
        kept = high.astype(F32) + low.astype(F32)
        sq_col[:, at] = jnp.sum(kept * kept, axis=0, keepdims=True) + 1e-06

    def reduced_row(factor):
        total = chunks_r[c]
        for offset in range(1, n_col):
            rs_r.wait_one(land_r, rs_r.peer(offset))
            total = total + land_r[rs_r.peer(offset)]
        return total[0:dim] * factor, total[dim : dim + 8]

    def finish(number, factor):
        share, misfit = reduced_row(factor)
        ag_r[c] = share
        gt_r.start_gather(ag_r)
        total = chunks_c[r]
        for offset in range(1, n_row):
            rs_c.wait_one(land_c, rs_c.peer(offset))
            total = total + land_c[rs_c.peer(offset)]
        ag_c[r, 0:dim] = total * factor
        ag_c[r, dim : dim + 8] = misfit
        gt_c.start_gather(ag_c)
        rs_r.wait_send(chunks_r)
        rs_c.wait_send(chunks_c)

        prepare_row(c, ag_r[c])
        prepare_col(r, ag_c[r, 0:dim])
        grand = ag_c[r, dim : dim + 8]
        for offset in range(1, n_col):
            peer = gt_r.peer(offset)
            gt_r.wait_one(ag_r, peer)
            prepare_row(peer, ag_r[peer])
        for offset in range(1, n_row):
            peer = gt_c.peer(offset)
            gt_c.wait_one(ag_c, peer)
            prepare_col(peer, ag_c[peer, 0:dim])
            grand = grand + ag_c[peer, dim : dim + 8]
        totals[number] = grand
        gt_r.wait_send(ag_r)
        gt_c.wait_send(ag_c)

    def tile_pass(more):
        acc_row[...] = jnp.zeros_like(acc_row)
        misfit_acc[...] = jnp.zeros((8, 128), F32)

        def add_row(at, high, low):
            contract = (((1,), (1,)), ((), ()))
            acc_row[...] += lax.dot_general(
                w_col[:, at], high, contract, preferred_element_type=F32
            ) + lax.dot_general(w_col[:, at], low, contract, preferred_element_type=F32)

        def late_step(step, carry):
            at = pl.ds(pl.multiple_of(step * STEP, STEP), STEP)
            add_row(at, *split(delta[:, at]))
            return carry

        def step_body(step, carry):
            at = pl.ds(pl.multiple_of(step * STEP, STEP), STEP)
            gram = jnp.dot(left[...], right[:, at], preferred_element_type=F32)
            squared = jnp.maximum(sq_row[...] + sq_col[:, at] + gram, 1e-06)
            inverse = lax.rsqrt(squared)
            tile = delta[:, at]
            error = jnp.where(tile > 0.0, tile - squared * inverse, 0.0)
            misfit_acc[...] += fold(error * error)
            if not more:
                delta[:, at] = tile * inverse
                return carry
            high, low = split(tile * inverse)
            add_row(at, high, low)
            weights = w_col[:, at]
            sums = jnp.dot(w_row[...], high, preferred_element_type=F32) + jnp.dot(
                w_row[...], low, preferred_element_type=F32
            )
            kept = weights[0:dim].astype(F32) + weights[dim : 2 * dim].astype(F32)
            part = sums[2 * dim : 2 * dim + 1] * kept - (sums[0:dim] + sums[dim : 2 * dim])
            for piece in range(STEP // blk):
                k = step * (STEP // blk) + piece
                chunks_c[k] = part[:, piece * blk : (piece + 1) * blk]

                @pl.when(k != r)
                def _():
                    rs_c.copy(chunks_c.at[k], land_c.at[r], k, r).start()

            return carry

        lax.fori_loop(0, cols // STEP, step_body, 0, unroll=UNROLL)
        misfit = misfit_acc[...]
        if not more:
            fin_c[r, 0:4] = misfit[0:4] + misfit[4:8]
            fin_c[r, 4:8] = scale_acc[0:4] + scale_acc[4:8]
            fn_c.start_gather(fin_c)
            lax.fori_loop(0, cols // STEP, late_step, 0, unroll=UNROLL)
        for k in range(n_col):
            at = slice(k * blk, (k + 1) * blk)
            kept = w_row[0:dim, at].astype(F32) + w_row[dim : 2 * dim, at].astype(F32)
            chunks_r[k, 0:dim] = acc_row[2 * dim : 2 * dim + 1, at] * kept - (
                acc_row[0:dim, at] + acc_row[dim : 2 * dim, at]
            )
            chunks_r[k, dim : dim + 8] = misfit
        rs_r.start_scatter(chunks_r, land_r)
        if not more:
            grand = fin_c[r]
            for offset in range(1, n_row):
                fn_c.wait_one(fin_c, fn_c.peer(offset))
                grand = grand + fin_c[fn_c.peer(offset)]
            fin_r[c] = grand
            fn_r.start_gather(fin_r)

    for k in range(n_col):
        prepare_row(k, pool[order_ref[r * n_col + k]])
    for k in range(n_row):
        prepare_col(k, pool[order_ref[c * n_row + k]])
    for copy in sent:
        copy.wait_send()

    def iteration(number, carry):
        tile_pass(True)
        finish(number, 1.0 / points)
        return carry

    lax.fori_loop(0, ITERS - 1, iteration, 0)
    tile_pass(False)
    share, _ = reduced_row(1.0 / points)
    out_ref[...] = share.T
    fn_r.wait_recv(fin_r)
    grand = fin_r[0]
    for k in range(1, n_col):
        grand = grand + fin_r[k]
    rs_r.wait_send(chunks_r)
    fn_r.wait_send(fin_r)
    fn_c.wait_send(fin_c)
    scale = jnp.sum(grand[4:8], keepdims=True)
    for number in range(ITERS):
        misfit = totals[number] if number < ITERS - 1 else grand[0:4]
        stress_ref[number] = (jnp.sum(misfit, keepdims=True) / scale)[0, 0]


def body(n_row, n_col, delta, coords, block_order):
    blk, dim = coords.shape
    rows, cols = delta.shape
    vmem = pl.BlockSpec(memory_space=pltpu.VMEM)
    return pl.pallas_call(
        functools.partial(kernel, n_row, n_col),
        out_shape=(
            jax.ShapeDtypeStruct((blk, dim), F32),
            jax.ShapeDtypeStruct((ITERS,), F32),
        ),
        in_specs=[
            pl.BlockSpec(memory_space=pltpu.SMEM),
            pl.BlockSpec(memory_space=pl.ANY),
            vmem,
        ],
        out_specs=(vmem, pl.BlockSpec(memory_space=pltpu.SMEM)),
        scratch_shapes=[
            pltpu.VMEM((rows, cols), F32),
            pltpu.VMEM((rows, 4 * dim), BF16),
            pltpu.VMEM((4 * dim, cols), BF16),
            pltpu.VMEM((2 * dim + 16, rows), BF16),
            pltpu.VMEM((2 * dim + 16, cols), BF16),
            pltpu.VMEM((rows, 1), F32),
            pltpu.VMEM((1, cols), F32),
            pltpu.VMEM((2 * dim + 16, rows), F32),
            pltpu.VMEM((n_col, dim + 8, blk), F32),
            pltpu.VMEM((n_row, dim, blk), F32),
            pltpu.VMEM((n_col, dim + 8, blk), F32),
            pltpu.VMEM((n_row, dim, blk), F32),
            pltpu.VMEM((n_col, dim, blk), F32),
            pltpu.VMEM((n_row, dim + 8, blk), F32),
            pltpu.VMEM((n_col, 8, 128), F32),
            pltpu.VMEM((n_row, 8, 128), F32),
            pltpu.VMEM((8, 128), F32),
            pltpu.VMEM((8, 128), F32),
            pltpu.VMEM((n_row * n_col, dim, blk), F32),
            pltpu.VMEM((ITERS, 8, 128), F32),
            pltpu.SemaphoreType.DMA,
            pltpu.SemaphoreType.DMA((n_row * n_col,)),
            pltpu.SemaphoreType.DMA((n_col,)),
            pltpu.SemaphoreType.DMA((n_row // 2, n_col)),
            pltpu.SemaphoreType.DMA((n_row // 2, n_col)),
            pltpu.SemaphoreType.DMA((6, n_col)),
            pltpu.SemaphoreType.DMA((6, n_row)),
        ],
        compiler_params=pltpu.CompilerParams(
            collective_id=0, has_side_effects=True, vmem_limit_bytes=48 * 1024 * 1024
        ),
    )(block_order, delta, coords)


def solution(mesh):
    sizes = dict(mesh.shape)
    return jax.shard_map(
        functools.partial(body, sizes["row"], sizes["col"]),
        mesh=mesh,
        in_specs=(P("row", "col"), P(("row", "col"), None), P()),
        out_specs=(P(("row", "col"), None), P()),
        check_vma=False,
    )
```

time: 81 us -> 70.9 us (0.88)
  Pallas kernels: 75.8 us -> 65.7 us
    pallas_call x1, Pallas kernels: 75.8 us -> 65.7 us  [body(): pl.pallas_call(functools.partial(kernel, n_row, n_col), out_shape=(jax.Sh...]
where the time goes in v2:
time: 70.9 us; the launch traced here: 70.6 us
  Pallas kernels  65.7 us (93%)
  local copies, waits for them, and re-layouts  4.3 us (6%)
    pallas_call x1, Pallas kernels, body(): pl.pallas_call(functools.partial(kernel, n_row, n_col), out_shape=(jax.Sh...  65.7 us
    unnamed x6, local copies, waits for them, and re-layouts  3.6 us

profile of v2, /device:TPU:0, one launch (start us, length us, event | category | flops | bytes accessed | tf_op | source)
XLA Modules:
  0.0 70.6 jit_solution(16198768759068081989)
XLA Ops:
  0.6 0.8 %copy.5.coords_ref = f32[128,64]{1,0:T(8,128)S(1)} copy(f32[128,64]{0,1:T(8,128)} %param.4) | data formatting | bytes 65536 | tf_op args[1]
  1.5 0.0 copy-start
  1.5 1.6 %copy-done = f32[512,1024]{1,0:T(8,128)S(1)} copy-done((f32[512,1024]{1,0:T(8,128)S(1)}, f32[512,1024]{1,0:T(8,128)}, u32[]{:S(2)}) %copy-start) | copy-done | bytes 2097176
  3.1 0.0 copy-start.1
  3.1 0.7 copy-done.1
  3.7 65.7 %shard_map.50 = (f32[128,64]{1,0:T(8,128)S(1)}, f32[4]{0:T(128)S(1)}) custom-call(s32[32]{0:T(128)S(1)} %copy-done.1, f32[512,1024]{1,0:T(8,128)S(1)} %copy-done, f32[128,64]{1,0:T(8,128)S(1)} %copy.5.coords_ref), custom_call_target="tpu_custom_call" | custom-call | tf_op jit(solution)/shard_map/pallas_call | solution.py:358
  69.4 0.7 copy.6
  70.1 0.5 copy.8
Async XLA Ops:
  1.5 1.6 %copy-start = (f32[512,1024]{1,0:T(8,128)S(1)}, f32[512,1024]{1,0:T(8,128)}, u32[]{:S(2)}) copy-start(f32[512,1024]{1,0:T(8,128)} %delta_hbm.1) | copy-start | bytes 6291460
  3.1 0.7 copy-start.1

commit v3 on v2

--- a/solution.py
+++ b/solution.py
@@ -12,7 +12,7 @@
 F32 = jnp.float32
 BF16 = jnp.bfloat16
 STEP = 512
-UNROLL = False
+UNROLL = True
 
 
 class Exchange:
@@ -218,52 +218,47 @@
         kept = high.astype(F32) + low.astype(F32)
         sq_col[:, at] = jnp.sum(kept * kept, axis=0, keepdims=True) + 1e-06
 
-    def reduced_row(factor):
-        total = chunks_r[c]
-        for offset in range(1, n_col):
-            rs_r.wait_one(land_r, rs_r.peer(offset))
-            total = total + land_r[rs_r.peer(offset)]
-        return total[0:dim] * factor, total[dim : dim + 8]
-
-    def finish(number, factor):
-        share, misfit = reduced_row(factor)
-        ag_r[c] = share
+    def reduced(exchange, chunks, landing, factor):
+        total = chunks[exchange.me]
+        for offset in range(1, exchange.size):
+            peer = exchange.peer(offset)
+            exchange.wait_one(landing, peer)
+            total = total + landing[peer]
+        return total * factor
+
+    def finish(factor):
+        ag_c[r] = reduced(rs_c, chunks_c, land_c, factor)
+        gt_c.start_gather(ag_c)
+        ag_r[c] = reduced(rs_r, chunks_r, land_r, factor)
         gt_r.start_gather(ag_r)
-        total = chunks_c[r]
-        for offset in range(1, n_row):
-            rs_c.wait_one(land_c, rs_c.peer(offset))
-            total = total + land_c[rs_c.peer(offset)]
-        ag_c[r, 0:dim] = total * factor
-        ag_c[r, dim : dim + 8] = misfit
-        gt_c.start_gather(ag_c)
+        prepare_col(r, ag_c[r])
+        prepare_row(c, ag_r[c])
         rs_r.wait_send(chunks_r)
         rs_c.wait_send(chunks_c)
-
-        prepare_row(c, ag_r[c])
-        prepare_col(r, ag_c[r, 0:dim])
-        grand = ag_c[r, dim : dim + 8]
+        for offset in range(1, n_row):
+            peer = gt_c.peer(offset)
+            gt_c.wait_one(ag_c, peer)
+            prepare_col(peer, ag_c[peer])
         for offset in range(1, n_col):
             peer = gt_r.peer(offset)
             gt_r.wait_one(ag_r, peer)
             prepare_row(peer, ag_r[peer])
-        for offset in range(1, n_row):
-            peer = gt_c.peer(offset)
-            gt_c.wait_one(ag_c, peer)
-            prepare_col(peer, ag_c[peer, 0:dim])
-            grand = grand + ag_c[peer, dim : dim + 8]
-        totals[number] = grand
         gt_r.wait_send(ag_r)
         gt_c.wait_send(ag_c)
 
-    def tile_pass(more):
+    def tile_pass(number, more):
         acc_row[...] = jnp.zeros_like(acc_row)
         misfit_acc[...] = jnp.zeros((8, 128), F32)
 
         def add_row(at, high, low):
             contract = (((1,), (1,)), ((), ()))
+            weights = w_col[:, at]
             acc_row[...] += lax.dot_general(
-                w_col[:, at], high, contract, preferred_element_type=F32
-            ) + lax.dot_general(w_col[:, at], low, contract, preferred_element_type=F32)
+                jnp.concatenate([weights, weights], axis=1),
+                jnp.concatenate([high, low], axis=1),
+                contract,
+                preferred_element_type=F32,
+            )
 
         def late_step(step, carry):
             at = pl.ds(pl.multiple_of(step * STEP, STEP), STEP)
@@ -301,18 +296,22 @@
 
         lax.fori_loop(0, cols // STEP, step_body, 0, unroll=UNROLL)
         misfit = misfit_acc[...]
-        if not more:
-            fin_c[r, 0:4] = misfit[0:4] + misfit[4:8]
-            fin_c[r, 4:8] = scale_acc[0:4] + scale_acc[4:8]
+        if more:
+            totals[number] = misfit
+        else:
+            sums = [jnp.sum(totals[k], axis=0, keepdims=True) for k in range(ITERS - 1)]
+            sums += [jnp.sum(misfit, axis=0, keepdims=True)]
+            sums += [jnp.sum(scale_acc[...], axis=0, keepdims=True)]
+            sums += [jnp.zeros((8 - len(sums), 128), F32)]
+            fin_c[r] = jnp.concatenate(sums, axis=0)
             fn_c.start_gather(fin_c)
             lax.fori_loop(0, cols // STEP, late_step, 0, unroll=UNROLL)
         for k in range(n_col):
             at = slice(k * blk, (k + 1) * blk)
             kept = w_row[0:dim, at].astype(F32) + w_row[dim : 2 * dim, at].astype(F32)
-            chunks_r[k, 0:dim] = acc_row[2 * dim : 2 * dim + 1, at] * kept - (
+            chunks_r[k] = acc_row[2 * dim : 2 * dim + 1, at] * kept - (
                 acc_row[0:dim, at] + acc_row[dim : 2 * dim, at]
             )
-            chunks_r[k, dim : dim + 8] = misfit
         rs_r.start_scatter(chunks_r, land_r)
         if not more:
             grand = fin_c[r]
@@ -330,13 +329,13 @@
         copy.wait_send()
 
     def iteration(number, carry):
-        tile_pass(True)
-        finish(number, 1.0 / points)
+        tile_pass(number, True)
+        finish(1.0 / points)
         return carry
 
     lax.fori_loop(0, ITERS - 1, iteration, 0)
-    tile_pass(False)
-    share, _ = reduced_row(1.0 / points)
+    tile_pass(ITERS - 1, False)
+    share = reduced(rs_r, chunks_r, land_r, 1.0 / points)
     out_ref[...] = share.T
     fn_r.wait_recv(fin_r)
     grand = fin_r[0]
@@ -345,10 +344,10 @@
     rs_r.wait_send(chunks_r)
     fn_r.wait_send(fin_r)
     fn_c.wait_send(fin_c)
-    scale = jnp.sum(grand[4:8], keepdims=True)
+    sums = jnp.sum(grand, axis=1, keepdims=True)
+    stress = sums / sums[ITERS : ITERS + 1]
     for number in range(ITERS):
-        misfit = totals[number] if number < ITERS - 1 else grand[0:4]
-        stress_ref[number] = (jnp.sum(misfit, keepdims=True) / scale)[0, 0]
+        stress_ref[number] = stress[number, 0]
 
 
 def body(n_row, n_col, delta, coords, block_order):
@@ -376,12 +375,12 @@
             pltpu.VMEM((rows, 1), F32),
             pltpu.VMEM((1, cols), F32),
             pltpu.VMEM((2 * dim + 16, rows), F32),
-            pltpu.VMEM((n_col, dim + 8, blk), F32),
-            pltpu.VMEM((n_row, dim, blk), F32),
-            pltpu.VMEM((n_col, dim + 8, blk), F32),
+            pltpu.VMEM((n_col, dim, blk), F32),
             pltpu.VMEM((n_row, dim, blk), F32),
             pltpu.VMEM((n_col, dim, blk), F32),
-            pltpu.VMEM((n_row, dim + 8, blk), F32),
+            pltpu.VMEM((n_row, dim, blk), F32),
+            pltpu.VMEM((n_col, dim, blk), F32),
+            pltpu.VMEM((n_row, dim, blk), F32),
             pltpu.VMEM((n_col, 8, 128), F32),
             pltpu.VMEM((n_row, 8, 128), F32),
             pltpu.VMEM((8, 128), F32),

time: 70.9 us -> 68.7 us (0.969)
  Pallas kernels: 65.7 us -> 63.6 us
    pallas_call x1, Pallas kernels: 65.7 us -> 63.6 us  [body(): pl.pallas_call(functools.partial(kernel, n_row, n_col), out_shape=(jax.Sh...]
where the time goes in v3:
time: 68.7 us; the launch traced here: 68.5 us
  Pallas kernels  63.6 us (93%)
  local copies, waits for them, and re-layouts  4.3 us (6%)
    pallas_call x1, Pallas kernels, body(): pl.pallas_call(functools.partial(kernel, n_row, n_col), out_shape=(jax.Sh...  63.6 us
    unnamed x6, local copies, waits for them, and re-layouts  3.6 us

profile of v3, /device:TPU:0, one launch (start us, length us, event | category | flops | bytes accessed | tf_op | source)
XLA Modules:
  0.0 68.5 jit_solution(5434936747327804985)
XLA Ops:
  0.6 0.8 %copy.5.coords_ref = f32[128,64]{1,0:T(8,128)S(1)} copy(f32[128,64]{0,1:T(8,128)} %param.4) | data formatting | bytes 65536 | tf_op args[1]
  1.5 0.0 copy-start
  1.5 1.6 %copy-done = f32[512,1024]{1,0:T(8,128)S(1)} copy-done((f32[512,1024]{1,0:T(8,128)S(1)}, f32[512,1024]{1,0:T(8,128)}, u32[]{:S(2)}) %copy-start) | copy-done | bytes 2097176
  3.1 0.0 copy-start.1
  3.1 0.7 copy-done.1
  3.7 63.6 %shard_map.50 = (f32[128,64]{1,0:T(8,128)S(1)}, f32[4]{0:T(128)S(1)}) custom-call(s32[32]{0:T(128)S(1)} %copy-done.1, f32[512,1024]{1,0:T(8,128)S(1)} %copy-done, f32[128,64]{1,0:T(8,128)S(1)} %copy.5.coords_ref), custom_call_target="tpu_custom_call" | custom-call | tf_op jit(solution)/shard_map/pallas_call | solution.py:357
  67.3 0.7 %copy.6 = f32[128,64]{0,1:T(8,128)} copy(f32[128,64]{1,0:T(8,128)S(1)} %get-tuple-element.2) | data formatting | bytes 65536 | tf_op jit(solution)/shard_map/pallas_call | solution.py:357
  68.0 0.5 copy.8
Async XLA Ops:
  1.5 1.6 %copy-start = (f32[512,1024]{1,0:T(8,128)S(1)}, f32[512,1024]{1,0:T(8,128)}, u32[]{:S(2)}) copy-start(f32[512,1024]{1,0:T(8,128)} %delta_hbm.1) | copy-start | bytes 6291460
  3.1 0.7 copy-start.1

commit v4 on v3

--- a/solution.py
+++ b/solution.py
@@ -202,8 +202,9 @@
         w_row[dim : 2 * dim, at] = low
         high, low = high.astype(F32), low.astype(F32)
         kept = high + low
-        stacked = jnp.concatenate([high, high, low, low], axis=0) * -2.0
-        left[at, :] = stacked.T.astype(BF16)
+        turned = (jnp.concatenate([high, low], axis=0) * -2.0).T.astype(BF16)
+        left[at, 0 : 2 * dim] = turned
+        left[at, 2 * dim : 4 * dim] = turned
         sq_row[at, :] = jnp.sum(kept * kept, axis=0, keepdims=True).T
 
     def prepare_col(k, block):
@@ -212,8 +213,8 @@
         w_col[0:dim, at] = high
         w_col[dim : 2 * dim, at] = low
         right[0:dim, at] = high
-        right[dim : 2 * dim, at] = low
-        right[2 * dim : 3 * dim, at] = high
+        right[dim : 2 * dim, at] = high
+        right[2 * dim : 3 * dim, at] = low
         right[3 * dim : 4 * dim, at] = low
         kept = high.astype(F32) + low.astype(F32)
         sq_col[:, at] = jnp.sum(kept * kept, axis=0, keepdims=True) + 1e-06
@@ -240,8 +241,9 @@
             gt_c.wait_one(ag_c, peer)
             prepare_col(peer, ag_c[peer])
         for offset in range(1, n_col):
+            gt_r.wait_one(ag_r, gt_r.peer(offset))
+        for offset in range(1, n_col):
             peer = gt_r.peer(offset)
-            gt_r.wait_one(ag_r, peer)
             prepare_row(peer, ag_r[peer])
         gt_r.wait_send(ag_r)
         gt_c.wait_send(ag_c)

time: 68.7 us -> 68.2 us (level)
  no operation moved by 1% of the time
where the time goes in v4:
time: 68.2 us; the launch traced here: 67.9 us
  Pallas kernels  63 us (92%)
  local copies, waits for them, and re-layouts  4.3 us (6%)
    pallas_call x1, Pallas kernels, body(): pl.pallas_call(functools.partial(kernel, n_row, n_col), out_shape=(jax.Sh...  63 us
    unnamed x6, local copies, waits for them, and re-layouts  3.6 us

profile of v4, /device:TPU:0, one launch (start us, length us, event | category | flops | bytes accessed | tf_op | source)
XLA Modules:
  0.0 67.9 jit_solution(1856850646102520426)
XLA Ops:
  0.6 0.8 %copy.5.coords_ref = f32[128,64]{1,0:T(8,128)S(1)} copy(f32[128,64]{0,1:T(8,128)} %param.4) | data formatting | bytes 65536 | tf_op args[1]
  1.5 0.0 copy-start
  1.5 1.6 %copy-done = f32[512,1024]{1,0:T(8,128)S(1)} copy-done((f32[512,1024]{1,0:T(8,128)S(1)}, f32[512,1024]{1,0:T(8,128)}, u32[]{:S(2)}) %copy-start) | copy-done | bytes 2097176
  3.1 0.0 copy-start.1
  3.1 0.7 copy-done.1
  3.7 63.0 %shard_map.50 = (f32[128,64]{1,0:T(8,128)S(1)}, f32[4]{0:T(128)S(1)}) custom-call(s32[32]{0:T(128)S(1)} %copy-done.1, f32[512,1024]{1,0:T(8,128)S(1)} %copy-done, f32[128,64]{1,0:T(8,128)S(1)} %copy.5.coords_ref), custom_call_target="tpu_custom_call" | custom-call | tf_op jit(solution)/shard_map/pallas_call | solution.py:359
  66.7 0.7 %copy.6 = f32[128,64]{0,1:T(8,128)} copy(f32[128,64]{1,0:T(8,128)S(1)} %get-tuple-element.2) | data formatting | bytes 65536 | tf_op jit(solution)/shard_map/pallas_call | solution.py:359
  67.4 0.5 copy.8
Async XLA Ops:
  1.5 1.6 %copy-start = (f32[512,1024]{1,0:T(8,128)S(1)}, f32[512,1024]{1,0:T(8,128)}, u32[]{:S(2)}) copy-start(f32[512,1024]{1,0:T(8,128)} %delta_hbm.1) | copy-start | bytes 6291460
  3.1 0.7 copy-start.1
